TPU v7x, 32 devices: a whole 2x2x4 slice. The times are simulated.
32 devices in a mesh: dp: 4 (over x, core), clique: 8 (over z, y).
Axes of the slice: x: 2, y: 2, z: 4, core: 2. Of those that a mesh axis runs over, the one named last changes fastest.
Arguments:
- table_rows: int32 [9, 262144], P(None, 'dp'), may hold values from 0 to 255
- attribute_order: int32 [9], replicated, may hold values from 0 to 8, each once
- log_potential: float32 [8, 256, 256], P('clique'), may hold values from -4 to 18
- measure_noise: float32 [8, 256, 256], P('clique'), may hold values from -24 to 24
Outputs:
- updated_potentials: float32 [8, 256, 256], P('clique')
- beliefs: float32 [8, 256, 256], P('clique')
Inputs may be any that keep to these rules, and one draw needn't show every extreme that they name: `attribute_order`: each of the 9 attributes appears once.
All inputs are finite; a program needn't handle non-finite values.
Results may differ from a plain program's by a relative error of at most 0.0003.
Values sent between devices are 32-bit elements; how exact they have to be, the bound alone decides.
A program may use at most 128 MiB of HBM per device.

v0:
```python
import functools
import math

import jax
import jax.numpy as jnp
from jax import lax
from jax.experimental import pallas as pl
from jax.experimental.pallas import tpu as pltpu
from jax.sharding import PartitionSpec as P

step_size = 0.25
PIECES = 4
BLOCK = 2048
QUARTERS = 4
MESH = pl.DeviceIdType.MESH
BF16 = jnp.bfloat16
F32 = jnp.float32
ONE = jnp.float8_e4m3fn


def split_high_low(value):
    high = value.astype(BF16)
    return high, (value - high.astype(F32)).astype(BF16)


def message_rows(vector):
    wide = jnp.broadcast_to(vector, (16, vector.shape[1]))
    high = wide.astype(BF16).astype(F32)
    row = lax.broadcasted_iota(jnp.int32, wide.shape, 0)
    return jnp.where(row < 8, high, wide - high).astype(BF16)


def carry(vector, kernel_high, kernel_low, contract):
    rows = message_rows(vector)
    dims = (((1,), (contract,)), ((), ()))
    moved = lax.dot_general(rows, kernel_high[...], dims, preferred_element_type=F32)
    moved += lax.dot_general(rows, kernel_low[...], dims, preferred_element_type=F32)
    return (moved[0:1] + moved[8:9]) / jnp.sum(vector)


def fill_one_hot(tab, attribute, start, levels, slot):
    kinds, deep, lanes = levels.shape
    width = slot.shape[1]
    values = tab[pl.ds(attribute, 1), pl.ds(pl.multiple_of(start, width), width)] - 128
    for tile in range(0, width, lanes):
        wide = jnp.broadcast_to(values[:, tile : tile + lanes], (deep, lanes))
        hit = wide.astype(jnp.int8)[None] == levels
        ones = jnp.where(hit, jnp.ones((), ONE), jnp.zeros((), ONE))
        slot[:, tile : tile + lanes] = ones.reshape(kinds * deep, lanes)


def kernel(
    sizes, scale, order, table, potential_in, noise_in, updated, beliefs,
    tabs, slots, potential, noise, acc, q, q_high, q_low, f_in, f_out, g_in, g_out, sibling, half, across, total,
    tab_sem, in_sem, f_sem, g_sem, send1, recv1, send2, recv2, send3, recv3,
):
    cliques, copies = sizes
    domain = q.shape[0]
    columns = tabs[0].shape[1]
    blocks = columns // BLOCK
    chips = copies // 2
    rows = domain // 2 // PIECES
    k = lax.axis_index("clique")
    d = lax.axis_index("dp")
    chip, core = d // 2, lax.rem(d, 2)
    twin = chip * 2 + 1 - core

    get_potential = pltpu.make_async_copy(potential_in.at[0], potential, in_sem.at[0])
    get_potential.start()
    loads = []
    for quarter, tab in enumerate(tabs):
        where = pl.ds(quarter * columns, columns)
        load = pltpu.make_async_copy(table.at[:, where], tab, tab_sem.at[quarter])
        load.start()
        loads.append(load)
    get_noise = pltpu.make_async_copy(noise_in.at[0], noise, in_sem.at[1])
    get_noise.start()

    barrier = pltpu.get_barrier_semaphore()

    def greet(device):
        pl.semaphore_signal(barrier, inc=1, device_id=device, device_id_type=MESH)

    greet({"dp": twin})
    for step in range(1, chips):
        greet({"dp": lax.rem(chip + step, chips) * 2 + core})

    @pl.when(k > 0)
    def _():
        greet({"clique": k - 1})

    @pl.when(k < cliques - 1)
    def _():
        greet({"clique": k + 1})

    get_potential.wait()
    q[...] = jnp.exp(potential[...])
    q_high[...], q_low[...] = split_high_low(q[...])
    acc[...] = jnp.zeros_like(acc)
    slots[1][0][...] = jnp.zeros_like(slots[1][0])
    slots[1][1][...] = jnp.zeros_like(slots[1][1])

    @pl.when(k == 0)
    def _():
        f_in[...] = jnp.ones_like(f_in)

    @pl.when(k == cliques - 1)
    def _():
        g_in[...] = jnp.ones_like(g_in)

    at_end = jnp.logical_or(k == 0, k == cliques - 1)

    @pl.when(at_end)
    def _():
        pl.semaphore_wait(barrier, chips + 1)

    @pl.when(jnp.logical_not(at_end))
    def _():
        pl.semaphore_wait(barrier, chips + 2)

    f_copy = pltpu.make_async_remote_copy(
        f_out, f_in, f_sem.at[0], f_sem.at[1], {"clique": lax.rem(k + 1, cliques)}, MESH
    )
    g_copy = pltpu.make_async_remote_copy(
        g_out, g_in, g_sem.at[0], g_sem.at[1],
        {"clique": lax.rem(k + cliques - 1, cliques)}, MESH,
    )

    def forward():
        @pl.when(k > 0)
        def _():
            f_copy.wait_recv()

        @pl.when(k < cliques - 1)
        def _():
            f_out[...] = carry(f_in[...], q_high, q_low, 0)
            f_copy.start()

    def backward():
        @pl.when(k < cliques - 1)
        def _():
            g_copy.wait_recv()

        @pl.when(k > 0)
        def _():
            g_out[...] = carry(g_in[...], q_high, q_low, 1)
            g_copy.start()

    left, right = order[k], order[k + 1]
    pairs = blocks // 2
    per = max(1, QUARTERS * pairs // cliques)
    shape = (domain // 32, 32, 128)
    level = lax.broadcasted_iota(jnp.int32, shape, 0) * 32
    level += lax.broadcasted_iota(jnp.int32, shape, 1)
    levels = (level - 128).astype(jnp.int8)

    def multiply(slot):
        acc[...] += lax.dot_general(
            slot[0][...], slot[1][...], (((1,), (1,)), ((), ())),
            preferred_element_type=F32,
        )

    for quarter, tab in enumerate(tabs):
        loads[quarter].wait()

        @pl.loop(0, pairs)
        def _(pair, tab=tab, quarter=quarter):
            for turn in range(2):
                start = (pair * 2 + turn) * BLOCK
                fill_one_hot(tab, left, start, levels, slots[turn][0])
                fill_one_hot(tab, right, start, levels, slots[turn][1])
                multiply(slots[1 - turn])
            done = quarter * pairs + pair
            pl.when(done == k * per)(forward)
            pl.when(done == (cliques - 1 - k) * per)(backward)

    multiply(slots[1])
    for late in range(QUARTERS * pairs, cliques):
        pl.when(k == late)(forward)
        pl.when(cliques - 1 - k == late)(backward)

    mine, theirs = core * (domain // 2), (1 - core) * (domain // 2)

    def part(base, piece):
        return pl.ds(pl.multiple_of(base + piece * rows, rows), rows)

    first_trip, second_trip, third_trip = [], [], []
    for piece in range(PIECES):
        copy = pltpu.make_async_remote_copy(
            acc.at[part(theirs, piece)], sibling.at[piece],
            send1.at[piece], recv1.at[piece], {"dp": twin}, MESH,
        )
        copy.start()
        first_trip.append(copy)
    for piece in range(PIECES):
        first_trip[piece].wait_recv()
        half[piece] = acc[part(mine, piece), :] + sibling[piece]
        for step in range(1, chips):
            copy = pltpu.make_async_remote_copy(
                half.at[piece], across.at[step - 1, piece],
                send2.at[step - 1, piece], recv2.at[step - 1, piece],
                {"dp": lax.rem(chip + step, chips) * 2 + core}, MESH,
            )
            copy.start()
            second_trip.append(copy)

    column = jnp.transpose(jnp.broadcast_to(f_in[...], (8, domain)))[:, 0:1]
    joint = (column / jnp.sum(f_in[...])) * q[...] * (g_in[...] / jnp.sum(g_in[...]))
    beliefs[...] = joint * (float(domain * domain) / jnp.sum(joint))

    get_noise.wait()

    def finish(where):
        measured = (total[where, :] + noise[where, :]) * scale
        updated[where, :] = potential[where, :] - step_size * (beliefs[where, :] - measured)

    for piece in range(PIECES):
        summed = half[piece]
        for step in range(1, chips):
            second_trip[piece * (chips - 1) + step - 1].wait_recv()
            summed = summed + across[step - 1, piece]
        total[part(mine, piece), :] = summed
        copy = pltpu.make_async_remote_copy(
            total.at[part(mine, piece)], total.at[part(mine, piece)],
            send3.at[piece], recv3.at[piece], {"dp": twin}, MESH,
        )
        copy.start()
        third_trip.append(copy)
        finish(part(mine, piece))
    for piece in range(PIECES):
        third_trip[piece].wait_recv()
        finish(part(theirs, piece))

    for copy in first_trip + second_trip + third_trip:
        copy.wait_send()

    @pl.when(k < cliques - 1)
    def _():
        f_copy.wait_send()

    @pl.when(k > 0)
    def _():
        g_copy.wait_send()


def per_device(table_rows, attribute_order, log_potential, measure_noise):
    cliques, copies = lax.axis_size("clique"), lax.axis_size("dp")
    domain = log_potential.shape[1]
    attributes, columns = table_rows.shape
    scale = domain * domain / (columns * copies)
    rows = domain // 2 // PIECES
    chips = copies // 2
    table = jax.ShapeDtypeStruct((domain, domain), F32)
    vmem = pl.BlockSpec(memory_space=pltpu.VMEM)
    hbm = pl.BlockSpec(memory_space=pl.ANY)
    dma = pltpu.SemaphoreType.DMA
    updated, beliefs = pl.pallas_call(
        functools.partial(kernel, (cliques, copies), scale),
        out_shape=(table, table),
        in_specs=[
            pl.BlockSpec(memory_space=pltpu.SMEM),
            hbm,
            hbm,
            hbm,
        ],
        out_specs=(vmem, vmem),
        scratch_shapes=[
            [pltpu.VMEM((attributes, columns // QUARTERS), jnp.int32)] * QUARTERS,
            [[pltpu.VMEM((domain, BLOCK), ONE)] * 2] * 2,
            pltpu.VMEM((domain, domain), F32),
            pltpu.VMEM((domain, domain), F32),
            pltpu.VMEM((domain, domain), F32),
            pltpu.VMEM((domain, domain), F32),
            pltpu.VMEM((domain, domain), BF16),
            pltpu.VMEM((domain, domain), BF16),
            pltpu.VMEM((1, domain), F32),
            pltpu.VMEM((1, domain), F32),
            pltpu.VMEM((1, domain), F32),
            pltpu.VMEM((1, domain), F32),
            pltpu.VMEM((PIECES, rows, domain), F32),
            pltpu.VMEM((PIECES, rows, domain), F32),
            pltpu.VMEM((chips - 1, PIECES, rows, domain), F32),
            pltpu.VMEM((domain, domain), F32),
            dma((QUARTERS,)),
            dma((2,)),
            dma((2,)),
            dma((2,)),
            dma((PIECES,)),
            dma((PIECES,)),
            dma((chips - 1, PIECES)),
            dma((chips - 1, PIECES)),
            dma((PIECES,)),
            dma((PIECES,)),
        ],
        compiler_params=pltpu.CompilerParams(
            collective_id=0, has_side_effects=True, vmem_limit_bytes=60 * 1024 * 1024
        ),
    )(attribute_order, table_rows, log_potential, measure_noise)
    return updated[None], beliefs[None]


def solution(mesh):
    in_specs = (P(None, "dp"), P(), P("clique", None, None), P("clique", None, None))
    out_specs = (P("clique", None, None), P("clique", None, None))
    return jax.shard_map(
        per_device, mesh=mesh, in_specs=in_specs, out_specs=out_specs, check_vma=False
    )
```

profile of v0, /device:TPU:1, one launch (start us, length us, event | category | flops | bytes accessed | tf_op | source)
XLA Modules:
  0.0 39.1 jit_solution(3979421431476421421)
XLA Ops:
  0.6 35.2 %shard_map.59 = (f32[256,256]{1,0:T(8,128)}, f32[256,256]{1,0:T(8,128)}) custom-call(s32[9]{0:T(128)} %order.1, s32[9,65536]{1,0:T(8,128)} %table.1, f32[1,256,256]{2,1,0:T(8,128)} %potential_in.1, f32[1,256,256]{2,1,0:T(8,128)} %noise_in.1), custom_call_target="tpu_custom_call" | custom-call | tf_op jit(solution)/shard_map/pallas_call | solution.py:257
  35.8 1.7 %copy.8 = f32[1,256,256]{2,1,0:T(8,128)} copy(f32[1,256,256]{2,1,0:T(8,128)} %bitcast.3) | data formatting | bytes 524288
  37.5 1.7 %copy.9 = f32[1,256,256]{2,1,0:T(8,128)} copy(f32[1,256,256]{2,1,0:T(8,128)} %bitcast.2) | data formatting | bytes 524288
where the time goes:
time: 39.5 us; the launch traced here: 39.1 us
  Pallas kernels  35.2 us (89%)
  local copies, waits for them, and re-layouts  3.34 us (8%)
  between operations  0.64 us (2%)
    pallas_call x1, Pallas kernels, per_device(): pl.pallas_call(functools.partial(kernel, (cliques, copies), scale), out_s...  35.2 us
    unnamed x2, local copies, waits for them, and re-layouts  3.34 us

commit v1 on v0

--- a/solution.py
+++ b/solution.py
@@ -12,6 +12,7 @@
 PIECES = 4
 BLOCK = 2048
 QUARTERS = 4
+MEET = 9
 MESH = pl.DeviceIdType.MESH
 BF16 = jnp.bfloat16
 F32 = jnp.float32
@@ -51,11 +52,14 @@
 
 def kernel(
     sizes, scale, order, table, potential_in, noise_in, updated, beliefs,
-    tabs, slots, potential, noise, acc, q, q_high, q_low, f_in, f_out, g_in, g_out, sibling, half, across, total,
-    tab_sem, in_sem, f_sem, g_sem, send1, recv1, send2, recv2, send3, recv3,
+    tabs, slots, potential, noise, acc, q, q_high, q_low, m_high, m_low,
+    vectors, sibling, half, across, total,
+    tab_sem, in_sem, pair_sem, f_sem, g_sem, send1, recv1, send2, recv2, send3, recv3,
 ):
     cliques, copies = sizes
-    domain = q.shape[0]
+    f_in, f_out, g_in, g_out, f_own, g_own = vectors
+    domain = acc.shape[0]
+    groups = cliques // 2
     columns = tabs[0].shape[1]
     blocks = columns // BLOCK
     chips = copies // 2
@@ -64,8 +68,12 @@
     d = lax.axis_index("dp")
     chip, core = d // 2, lax.rem(d, 2)
     twin = chip * 2 + 1 - core
-
-    get_potential = pltpu.make_async_copy(potential_in.at[0], potential, in_sem.at[0])
+    group, odd = k // 2, lax.rem(k, 2)
+    partner = group * 2 + 1 - odd
+
+    get_potential = pltpu.make_async_copy(
+        potential_in.at[0], potential.at[odd], in_sem.at[0]
+    )
     get_potential.start()
     loads = []
     for quarter, tab in enumerate(tabs):
@@ -85,70 +93,86 @@
     for step in range(1, chips):
         greet({"dp": lax.rem(chip + step, chips) * 2 + core})
 
-    @pl.when(k > 0)
-    def _():
-        greet({"clique": k - 1})
-
-    @pl.when(k < cliques - 1)
-    def _():
-        greet({"clique": k + 1})
-
-    get_potential.wait()
-    q[...] = jnp.exp(potential[...])
-    q_high[...], q_low[...] = split_high_low(q[...])
+    greet({"clique": partner})
+
+    @pl.when(group > 0)
+    def _():
+        greet({"clique": k - 2})
+
+    @pl.when(group < groups - 1)
+    def _():
+        greet({"clique": k + 2})
+
     acc[...] = jnp.zeros_like(acc)
     slots[1][0][...] = jnp.zeros_like(slots[1][0])
     slots[1][1][...] = jnp.zeros_like(slots[1][1])
 
-    @pl.when(k == 0)
+    @pl.when(group == 0)
     def _():
         f_in[...] = jnp.ones_like(f_in)
 
-    @pl.when(k == cliques - 1)
+    @pl.when(group == groups - 1)
     def _():
         g_in[...] = jnp.ones_like(g_in)
 
-    at_end = jnp.logical_or(k == 0, k == cliques - 1)
+    at_end = jnp.logical_or(group == 0, group == groups - 1)
 
     @pl.when(at_end)
     def _():
-        pl.semaphore_wait(barrier, chips + 1)
+        pl.semaphore_wait(barrier, chips + 2)
 
     @pl.when(jnp.logical_not(at_end))
     def _():
-        pl.semaphore_wait(barrier, chips + 2)
-
+        pl.semaphore_wait(barrier, chips + 3)
+
+    pair_copy = pltpu.make_async_remote_copy(
+        potential_in.at[0], potential.at[odd], pair_sem.at[0], pair_sem.at[1],
+        {"clique": partner}, MESH,
+    )
+    pair_copy.start()
     f_copy = pltpu.make_async_remote_copy(
-        f_out, f_in, f_sem.at[0], f_sem.at[1], {"clique": lax.rem(k + 1, cliques)}, MESH
+        f_out, f_in, f_sem.at[0], f_sem.at[1], {"clique": lax.rem(k + 2, cliques)}, MESH
     )
     g_copy = pltpu.make_async_remote_copy(
         g_out, g_in, g_sem.at[0], g_sem.at[1],
-        {"clique": lax.rem(k + cliques - 1, cliques)}, MESH,
-    )
-
-    def forward():
-        @pl.when(k > 0)
+        {"clique": lax.rem(k + cliques - 2, cliques)}, MESH,
+    )
+
+    def prepare(which):
+        q[which] = jnp.exp(potential[which])
+        q_high[which], q_low[which] = split_high_low(q[which])
+
+    get_potential.wait()
+    prepare(odd)
+
+    def pair_product():
+        pair_copy.wait_recv()
+        prepare(1 - odd)
+        product = jnp.dot(q_high[0], q_high[1], preferred_element_type=F32)
+        product += jnp.dot(q_high[0], q_low[1], preferred_element_type=F32)
+        product += jnp.dot(q_low[0], q_high[1], preferred_element_type=F32)
+        m_high[...], m_low[...] = split_high_low(product)
+
+    def stage(number):
+        @pl.when(group == number)
         def _():
-            f_copy.wait_recv()
-
-        @pl.when(k < cliques - 1)
+            if number > 0:
+                f_copy.wait_recv()
+            if number < groups - 1:
+                f_out[...] = carry(f_in[...], m_high, m_low, 0)
+                f_copy.start()
+
+        @pl.when(group == groups - 1 - number)
         def _():
-            f_out[...] = carry(f_in[...], q_high, q_low, 0)
-            f_copy.start()
-
-    def backward():
-        @pl.when(k < cliques - 1)
-        def _():
-            g_copy.wait_recv()
-
-        @pl.when(k > 0)
-        def _():
-            g_out[...] = carry(g_in[...], q_high, q_low, 1)
-            g_copy.start()
+            if number > 0:
+                g_copy.wait_recv()
+            if number < groups - 1:
+                g_out[...] = carry(g_in[...], m_high, m_low, 1)
+                g_copy.start()
 
     left, right = order[k], order[k + 1]
     pairs = blocks // 2
-    per = max(1, QUARTERS * pairs // cliques)
+    meet = min(MEET, QUARTERS * pairs - 1)
     shape = (domain // 32, 32, 128)
     level = lax.broadcasted_iota(jnp.int32, shape, 0) * 32
     level += lax.broadcasted_iota(jnp.int32, shape, 1)
@@ -170,15 +194,13 @@
                 fill_one_hot(tab, left, start, levels, slots[turn][0])
                 fill_one_hot(tab, right, start, levels, slots[turn][1])
                 multiply(slots[1 - turn])
-            done = quarter * pairs + pair
-            pl.when(done == k * per)(forward)
-            pl.when(done == (cliques - 1 - k) * per)(backward)
+
+            @pl.when(quarter * pairs + pair == meet)
+            def _():
+                pair_product()
+                stage(0)
 
     multiply(slots[1])
-    for late in range(QUARTERS * pairs, cliques):
-        pl.when(k == late)(forward)
-        pl.when(cliques - 1 - k == late)(backward)
-
     mine, theirs = core * (domain // 2), (1 - core) * (domain // 2)
 
     def part(base, piece):
@@ -192,6 +214,8 @@
         )
         copy.start()
         first_trip.append(copy)
+    for number in range(1, groups - 2):
+        stage(number)
     for piece in range(PIECES):
         first_trip[piece].wait_recv()
         half[piece] = acc[part(mine, piece), :] + sibling[piece]
@@ -204,15 +228,9 @@
             copy.start()
             second_trip.append(copy)
 
-    column = jnp.transpose(jnp.broadcast_to(f_in[...], (8, domain)))[:, 0:1]
-    joint = (column / jnp.sum(f_in[...])) * q[...] * (g_in[...] / jnp.sum(g_in[...]))
-    beliefs[...] = joint * (float(domain * domain) / jnp.sum(joint))
-
+    for number in range(max(1, groups - 2), groups - 1):
+        stage(number)
     get_noise.wait()
-
-    def finish(where):
-        measured = (total[where, :] + noise[where, :]) * scale
-        updated[where, :] = potential[where, :] - step_size * (beliefs[where, :] - measured)
 
     for piece in range(PIECES):
         summed = half[piece]
@@ -226,6 +244,30 @@
         )
         copy.start()
         third_trip.append(copy)
+
+    if groups > 1:
+        stage(groups - 1)
+
+    @pl.when(odd == 1)
+    def _():
+        f_own[...] = carry(f_in[...], q_high.at[0], q_low.at[0], 0)
+        g_own[...] = g_in[...]
+
+    @pl.when(odd == 0)
+    def _():
+        f_own[...] = f_in[...]
+        g_own[...] = carry(g_in[...], q_high.at[1], q_low.at[1], 1)
+
+    f, g = f_own[...], g_own[...]
+    column = jnp.transpose(jnp.broadcast_to(f / jnp.sum(f), (8, domain)))[:, 0:1]
+    joint = column * q[odd] * (g / jnp.sum(g))
+    beliefs[...] = joint * (float(domain * domain) / jnp.sum(joint))
+
+    def finish(where):
+        measured = (total[where, :] + noise[where, :]) * scale
+        updated[where, :] = potential[odd, where, :] - step_size * (beliefs[where, :] - measured)
+
+    for piece in range(PIECES):
         finish(part(mine, piece))
     for piece in range(PIECES):
         third_trip[piece].wait_recv()
@@ -234,11 +276,13 @@
     for copy in first_trip + second_trip + third_trip:
         copy.wait_send()
 
-    @pl.when(k < cliques - 1)
+    pair_copy.wait_send()
+
+    @pl.when(group < groups - 1)
     def _():
         f_copy.wait_send()
 
-    @pl.when(k > 0)
+    @pl.when(group > 0)
     def _():
         g_copy.wait_send()
 
@@ -267,21 +311,21 @@
         scratch_shapes=[
             [pltpu.VMEM((attributes, columns // QUARTERS), jnp.int32)] * QUARTERS,
             [[pltpu.VMEM((domain, BLOCK), ONE)] * 2] * 2,
+            pltpu.VMEM((2, domain, domain), F32),
             pltpu.VMEM((domain, domain), F32),
             pltpu.VMEM((domain, domain), F32),
-            pltpu.VMEM((domain, domain), F32),
-            pltpu.VMEM((domain, domain), F32),
+            pltpu.VMEM((2, domain, domain), F32),
+            pltpu.VMEM((2, domain, domain), BF16),
+            pltpu.VMEM((2, domain, domain), BF16),
             pltpu.VMEM((domain, domain), BF16),
             pltpu.VMEM((domain, domain), BF16),
-            pltpu.VMEM((1, domain), F32),
-            pltpu.VMEM((1, domain), F32),
-            pltpu.VMEM((1, domain), F32),
-            pltpu.VMEM((1, domain), F32),
+            [pltpu.VMEM((1, domain), F32)] * 6,
             pltpu.VMEM((PIECES, rows, domain), F32),
             pltpu.VMEM((PIECES, rows, domain), F32),
             pltpu.VMEM((chips - 1, PIECES, rows, domain), F32),
             pltpu.VMEM((domain, domain), F32),
             dma((QUARTERS,)),
+            dma((2,)),
             dma((2,)),
             dma((2,)),
             dma((2,)),

time: 39.5 us -> 27.8 us (0.70)
  the two profiles are of different devices: /device:TPU:1 before, /device:TPU:0 now
where the time goes in v1:
time: 27.8 us; the launch traced here: 27.6 us
  Pallas kernels  23.6 us (85%)
  local copies, waits for them, and re-layouts  3.34 us (12%)
  between operations  0.64 us (2%)
    pallas_call x1, Pallas kernels, per_device(): pl.pallas_call(functools.partial(kernel, (cliques, copies), scale), out_s...  23.6 us
    unnamed x2, local copies, waits for them, and re-layouts  3.34 us

profile of v1, /device:TPU:0, one launch (start us, length us, event | category | flops | bytes accessed | tf_op | source)
XLA Modules:
  0.0 27.6 jit_solution(1472920830448460179)
XLA Ops:
  0.6 23.6 %shard_map.59 = (f32[256,256]{1,0:T(8,128)}, f32[256,256]{1,0:T(8,128)}) custom-call(s32[9]{0:T(128)} %order.1, s32[9,65536]{1,0:T(8,128)} %table.1, f32[1,256,256]{2,1,0:T(8,128)} %potential_in.1, f32[1,256,256]{2,1,0:T(8,128)} %noise_in.1), custom_call_target="tpu_custom_call" | custom-call | tf_op jit(solution)/shard_map/pallas_call | solution.py:301
  24.3 1.7 %copy.8 = f32[1,256,256]{2,1,0:T(8,128)} copy(f32[1,256,256]{2,1,0:T(8,128)} %bitcast.3) | data formatting | bytes 524288
  26.0 1.7 %copy.9 = f32[1,256,256]{2,1,0:T(8,128)} copy(f32[1,256,256]{2,1,0:T(8,128)} %bitcast.2) | data formatting | bytes 524288
